TPU v7x, 32 devices: a whole 2x2x4 slice. The times are simulated.
32 devices in a mesh: doc: 8 (over z, y), feat: 4 (over x, core).
Axes of the slice: x: 2, y: 2, z: 4, core: 2. Of those that a mesh axis runs over, the one named last changes fastest.
Arguments:
- scores: float32 [96, 128], P('doc'), may hold values from -6 to 6
- clicks: int32 [96, 128], P('doc'), may hold values from 0 to 1, as said below
- lengths: int32 [96], P('doc'), may hold values from 2 to 128, as said below
- t_plus_old: float32 [128], replicated, may hold values from 0.1 to 1
- t_minus_old: float32 [128], replicated, may hold values from 0.1 to 1
- leaf: int32 [12288], P('doc'), may hold values from 0 to 31
- bins: int32 [512, 12288], P('feat', 'doc'), may hold values from 0 to 255
Outputs:
- t_plus: float32 [128], replicated
- t_minus: float32 [128], replicated
- gradients: float32 [2, 12288], P(None, 'doc')
- hist: float32 [512, 64, 256], P(('feat', 'doc'))
Inputs may be any that keep to these rules, and one draw needn't show every extreme that they name: Query q shows its first lengths[q] slots; the first two queries of each block of 12 queries show all 128. `clicks`: values at or beyond a query's length carry no meaning. In the first query of each block of 12 queries the even positions are clicked and the odd ones not; in the second the reverse.
All inputs are finite; a program needn't handle non-finite values.
Results may differ from a plain program's by a relative error of at most 0.0024.
Values may be sent and summed in bfloat16 or wider, within the bound.
A program may use at most 64 MiB of HBM per device.

v0:
```python
import math

import jax
import jax.numpy as jnp
from jax import lax
from jax.sharding import PartitionSpec as P

BINS = 256
LEAVES = 32


def pair_terms(scores, clicks, lengths, t_plus_old, t_minus_old):
    npos = scores.shape[1]
    places = jnp.arange(npos)
    shown_mask = places[None, :] < lengths[:, None]
    clicked = jnp.where((clicks == 1) & shown_mask, 1.0, 0.0).astype(jnp.float32)
    skipped = jnp.where((clicks == 0) & shown_mask, 1.0, 0.0).astype(jnp.float32)
    paired = clicked[:, :, None] * skipped[:, None, :]
    discount = 1.0 / jnp.log2(2.0 + places.astype(jnp.float32))
    clicks_count = jnp.sum(clicked, axis=1)
    ideal_gain = jnp.sum(
        jnp.where(
            places[None, :].astype(jnp.float32) < clicks_count[:, None], discount[None, :], 0.0
        ),
        axis=1,
    )
    ideal_gain = jnp.maximum(ideal_gain, 1.0)
    change = (
        paired * jnp.abs(discount[:, None] - discount[None, :])[None] / ideal_gain[:, None, None]
    )
    spread = scores[:, :, None] - scores[:, None, :]
    weighted = change * jax.nn.softplus(-spread)
    plus_part = jnp.sum(weighted / t_minus_old[None, None, :], axis=(0, 2))
    minus_part = jnp.sum(weighted / t_plus_old[None, :, None], axis=(0, 1))
    return (change, spread, plus_part, minus_part)


def lambda_rows(change, spread, plus_sum, minus_sum):
    t_plus = jnp.sqrt(plus_sum / plus_sum[0])
    t_minus = jnp.sqrt(minus_sum / minus_sum[0])
    scaled = change / (t_plus[None, :, None] * t_minus[None, None, :])
    chance = jax.nn.sigmoid(-spread)
    lambda_pair = scaled * chance
    second = lambda_pair * (1.0 - chance)
    slopes = jnp.sum(lambda_pair, axis=1) - jnp.sum(lambda_pair, axis=2)
    curvature = jnp.sum(second, axis=1) + jnp.sum(second, axis=2)
    own_rows = jnp.stack([slopes.reshape(-1), curvature.reshape(-1)])
    return (t_plus, t_minus, own_rows)


def leaf_weights(slope_row, curve_row, leaf_row):
    leaf_hit = (leaf_row[None, :] == jnp.arange(LEAVES)[:, None]).astype(jnp.bfloat16)
    return jnp.concatenate([leaf_hit * slope_row[None, :], leaf_hit * curve_row[None, :]], axis=0)


def block_hist(bin_rows, weights, levels):
    one_hot = (bin_rows[:, None, :] == levels[None, :, None]).astype(jnp.bfloat16)
    return jnp.einsum("gr,nbr->ngb", weights, one_hot, preferred_element_type=jnp.float32)


def body(scores, clicks, lengths, t_plus_old, t_minus_old, leaf, bins):
    per_feat = scores.shape[0] // lax.axis_size("feat")
    start_row = lax.axis_index("feat") * per_feat
    my_scores = lax.dynamic_slice_in_dim(scores, start_row, per_feat, 0)
    my_clicks = lax.dynamic_slice_in_dim(clicks, start_row, per_feat, 0)
    my_lengths = lax.dynamic_slice_in_dim(lengths, start_row, per_feat, 0)
    change, spread, plus_part, minus_part = pair_terms(
        my_scores, my_clicks, my_lengths, t_plus_old, t_minus_old
    )
    plus_sum, minus_sum = lax.psum((plus_part, minus_part), ("doc", "feat"))
    t_plus, t_minus, own_rows = lambda_rows(change, spread, plus_sum, minus_sum)
    gradients = lax.all_gather(own_rows, "feat", axis=1, tiled=True)
    rounded = gradients.astype(jnp.bfloat16)
    columns_all = lax.all_to_all(
        bins.astype(jnp.bfloat16), "doc", split_axis=0, concat_axis=1, tiled=True
    )
    packed = jnp.stack([rounded[0], rounded[1], leaf.astype(jnp.bfloat16)])
    levels = jnp.arange(BINS, dtype=jnp.int32).astype(jnp.bfloat16)
    empty = jnp.zeros((columns_all.shape[0], 2 * LEAVES, BINS), jnp.float32)
    piece = lax.all_gather(packed, "doc", axis=1, tiled=True)
    piece_rows = piece.shape[1]
    block_size = math.gcd(piece_rows, 8192)

    def one_step(step_index, running):
        offset = (step_index * block_size).astype(jnp.int32)
        portion = lax.dynamic_slice_in_dim(piece, offset, block_size, 1)
        columns = lax.dynamic_slice_in_dim(columns_all, offset, block_size, 1)
        weights = leaf_weights(portion[0], portion[1], portion[2].astype(jnp.int32))
        return running + block_hist(columns, weights, levels)

    hist = lax.fori_loop(0, piece_rows // block_size, one_step, empty)
    return (t_plus, t_minus, gradients, hist)


def solution(mesh):
    placed = (P("doc", None), P("doc", None), P("doc"), P(), P(), P("doc"), P("feat", "doc"))
    return jax.shard_map(
        body,
        mesh=mesh,
        in_specs=placed,
        out_specs=(P(), P(), P(None, "doc"), P(("feat", "doc"), None, None)),
        check_vma=False,
    )
```

profile of v0, /device:TPU:0, one launch (start us, length us, event | category | flops | bytes accessed | tf_op | source)
XLA Modules:
  0.0 132.6 jit_solution(1292160060614827381)
XLA Ops:
  0.6 0.0 copy-start.3
  0.6 0.0 copy-start.5
  0.7 0.0 copy-start.4
  0.7 0.0 copy-start
  0.7 1.9 %convert_element_type.45 = bf16[128,1536]{1,0:T(8,128)(2,1)} convert(s32[128,1536]{1,0:T(8,128)} %param.15) | non-fusion elementwise | flops 196608 | bytes 1179648 | tf_op jit(solution)/shard_map/convert_element_type | solution.py:75
  2.6 7.3 %all-to-all-start = ((bf16[8,16,1536]{2,1,0:T(8,128)(2,1)}), bf16[8,16,1536]{2,1,0:T(8,128)(2,1)S(1)}, u32[]{:S(2)}, u32[]{:S(2)}) async-start(bf16[8,16,1536]{2,1,0:T(8,128)(2,1)} %bitcast.2), calls=%async_computation | async-start | bytes 786432 | tf_op jit(solution)/shard_map/all_to_all | solution.py:74
  9.9 0.1 subtract_abs_fusion
  10.0 0.0 copy-done.3
  10.0 0.1 dynamic_slice.24
  10.1 0.9 fusion.34
  11.0 0.2 select_reduce_fusion
  11.2 0.0 copy-done.5
  11.2 0.0 copy-done.4
  11.2 0.3 divide_reduce_fusion
  11.5 41.1 %all-reduce = (f32[128]{0:T(128)S(1)}, f32[128]{0:T(128)S(1)}) all-reduce(f32[128]{0:T(128)S(1)} %get-tuple-element.123, f32[128]{0:T(128)S(1)} %get-tuple-element.122), channel_id=1, replica_groups=mesh['doc'=8,'feat'=4] {'doc','feat'}, use_global_device_ids=true, to_apply=%region_3.4 | all-reduce | flops 256 | bytes 2048 | tf_op jit(solution)/shard_map/psum | solution.py:70
  52.7 0.0 copy-start.1
  52.8 0.0 copy-start.2
  52.8 0.1 broadcast_multiply_fusion
  52.9 0.3 fusion.26
  53.3 5.5 %all_gather.6 = f32[2,1536]{1,0:T(2,128)S(1)} all-gather(f32[2,384]{1,0:T(2,128)S(1)} %pad_maximum_fusion.1), channel_id=1, replica_groups=mesh['doc'=8,'feat'=4] {'feat'}, dimensions={1}, use_global_device_ids=true | all-gather | bytes 15360 | tf_op jit(solution)/shard_map/all_gather | solution.py:72
  58.8 0.0 copy-done
  58.8 30.5 %all_gather.7 = bf16[3,12288]{1,0:T(4,128)(2,1)S(1)} all-gather(bf16[3,1536]{1,0:T(4,128)(2,1)S(1)} %pad_maximum_fusion), channel_id=1, replica_groups=mesh['doc'=8,'feat'=4] {'doc'}, dimensions={1}, use_global_device_ids=true | all-gather | bytes 82944 | tf_op jit(solution)/shard_map/all_gather | solution.py:80
  89.4 0.0 all-to-all-done
  89.4 0.0 copy-done.1
  89.4 0.0 copy-done.2
  89.4 42.2 %while.14 = (s32[]{:T(128)}, f32[16,64,256]{2,1,0:T(8,128)S(1)}, bf16[16,12288]{1,0:T(8,128)(2,1)S(1)}, bf16[3,12288]{1,0:T(4,128)(2,1)S(1)}, s32[]{:T(128)}, /*...) while((s32[]{:T(128)}, f32[16,64,256]{2,1,0:T(8,128)S(1)}, bf16[16,12288]{1,0:T(8,128)(2,1)S(1)}, ...), condition=%wide.region_11.12_spmd.clone, body=%wide.region_10.11_spmd.clone.sunk | while | flops 2166231296 | bytes 3630285 | solution.py:91
  89.5 0.1 dynamic-slice_reduce_fusion.3
  89.6 0.1 fusion.40
  89.7 13.8 %fusion.41 = f32[16,64,256]{2,1,0:T(8,128)S(1)} fusion(bf16[16,4096]{1,0:T(8,128)(2,1)S(1)} %constant_dynamic-slice_fusion.3, bf16[256]{0:T(256)(128)(2,1)S(1)} %iota_convert_fusion.3, f32[16,64,256]{2,1,0:T(8,128)S(1)} %get-tuple-element.187, bf16[32,4096]{1,0:T(8,128)(2,1)S(1)} %get-tuple-element.174, bf16[32,4096]{1,0:T(8,128)(2,1)S(1)} %get-tuple-element.175, ...), kind=kOutput, calls=%fused_computation.6.clone.1 | convolution fusion | flops 2165833728 | bytes 2753025 | tf_op jit(solution)/shard_map/while/body/eval_jaxpr/gr,nbr->ngb/dot_general | solution.py:58
  103.5 0.1 dynamic-slice_reduce_fusion.3
  103.7 0.1 fusion.40
  103.8 13.8 %fusion.41 = f32[16,64,256]{2,1,0:T(8,128)S(1)} fusion(bf16[16,4096]{1,0:T(8,128)(2,1)S(1)} %constant_dynamic-slice_fusion.3, bf16[256]{0:T(256)(128)(2,1)S(1)} %iota_convert_fusion.3, f32[16,64,256]{2,1,0:T(8,128)S(1)} %get-tuple-element.187, bf16[32,4096]{1,0:T(8,128)(2,1)S(1)} %get-tuple-element.174, bf16[32,4096]{1,0:T(8,128)(2,1)S(1)} %get-tuple-element.175, ...), kind=kOutput, calls=%fused_computation.6.clone.1 | convolution fusion | flops 2165833728 | bytes 2753025 | tf_op jit(solution)/shard_map/while/body/eval_jaxpr/gr,nbr->ngb/dot_general | solution.py:58
  117.6 0.1 dynamic-slice_reduce_fusion.3
  117.8 0.1 fusion.40
  117.9 13.8 %fusion.41 = f32[16,64,256]{2,1,0:T(8,128)S(1)} fusion(bf16[16,4096]{1,0:T(8,128)(2,1)S(1)} %constant_dynamic-slice_fusion.3, bf16[256]{0:T(256)(128)(2,1)S(1)} %iota_convert_fusion.3, f32[16,64,256]{2,1,0:T(8,128)S(1)} %get-tuple-element.187, bf16[32,4096]{1,0:T(8,128)(2,1)S(1)} %get-tuple-element.174, bf16[32,4096]{1,0:T(8,128)(2,1)S(1)} %get-tuple-element.175, ...), kind=kOutput, calls=%fused_computation.6.clone.1 | convolution fusion | flops 2165833728 | bytes 2753025 | tf_op jit(solution)/shard_map/while/body/eval_jaxpr/gr,nbr->ngb/dot_general | solution.py:58
  131.6 0.0 copy-start.6
  131.7 0.6 copy.28
  132.3 0.3 copy-done.6
  (22 shorter events, 0.3 us)
Async XLA Ops:
  0.6 9.4 %copy-start.3 = (s32[12]{0:T(128)S(1)}, s32[12]{0:T(128)}, u32[]{:S(2)}) copy-start(s32[12]{0:T(128)} %param.11) | copy-start | bytes 148
  0.6 10.6 %copy-start.5 = (f32[128]{0:T(128)S(1)}, f32[128]{0:T(128)}, u32[]{:S(2)}) copy-start(f32[128]{0:T(128)} %param.13) | copy-start | bytes 1540
  0.7 10.5 %copy-start.4 = (f32[128]{0:T(128)S(1)}, f32[128]{0:T(128)}, u32[]{:S(2)}) copy-start(f32[128]{0:T(128)} %param.12) | copy-start | bytes 1540
  0.7 58.1 %copy-start = (s32[1536]{0:T(1024)S(1)}, s32[1536]{0:T(1024)}, u32[]{:S(2)}) copy-start(s32[1536]{0:T(1024)} %param.14) | copy-start | bytes 18436
  2.6 86.8 %all-to-all-start = ((bf16[8,16,1536]{2,1,0:T(8,128)(2,1)}), bf16[8,16,1536]{2,1,0:T(8,128)(2,1)S(1)}, u32[]{:S(2)}, u32[]{:S(2)}) async-start(bf16[8,16,1536]{2,1,0:T(8,128)(2,1)} %bitcast.2), calls=%async_computation | async-start | bytes 786432 | tf_op jit(solution)/shard_map/all_to_all | solution.py:74
  52.7 36.7 %copy-start.1 = (f32[128]{0:T(128)}, f32[128]{0:T(128)S(1)}, u32[]{:S(2)}) copy-start(f32[128]{0:T(128)S(1)} %divide_sqrt_fusion.1) | copy-start | bytes 1540
  52.8 36.7 %copy-start.2 = (f32[128]{0:T(128)}, f32[128]{0:T(128)S(1)}, u32[]{:S(2)}) copy-start(f32[128]{0:T(128)S(1)} %divide_sqrt_fusion) | copy-start | bytes 1540
  131.6 1.0 copy-start.6
where the time goes:
time: 133 us
  blocking collectives  77.2 us (58%)
  matrix products  41.3 us (31%)
  starting transfers between devices  7.28 us (5%)
  other arithmetic  4.7 us (4%)
    dot_general x3, matrix products, block_hist(): jnp.einsum('gr,nbr->ngb', weights, one_hot, preferred_element_type=jnp.fl...  41.3 us
    psum x1, blocking collectives, body(): plus_sum, minus_sum = lax.psum((plus_part, minus_part), ('doc', 'feat'))  41.1 us
    all_gather x1, blocking collectives, body(): piece = lax.all_gather(packed, 'doc', axis=1, tiled=True)  30.5 us
    all_to_all x1, starting transfers between devices, body(): lax.all_to_all(bins.astype(jnp.bfloat16), 'doc', split_axis=0, concat_axi...  7.28 us
    all_gather x1, blocking collectives, body(): gradients = lax.all_gather(own_rows, 'feat', axis=1, tiled=True)  5.5 us
  transfers between devices with their start and end apart: 1, of which 0 were waited for; matrix products, arithmetic and copies ran while one was open for 2% of the time, Pallas kernels for 0%

commit v1 on v0

v1 whole, which is shorter than its diff:
```python
import functools

import jax
import jax.numpy as jnp
from jax import lax
from jax.experimental import pallas as pl
from jax.experimental.pallas import tpu as pltpu
from jax.sharding import PartitionSpec as P

BINS = 256
LEAVES = 32
F8 = jnp.float8_e4m3fn
BF = jnp.bfloat16
F32 = jnp.float32
MESH = pl.DeviceIdType.MESH
NT = (((1,), (1,)), ((), ()))


def rows_kernel(
    ndoc,
    scores_ref,
    clicks_ref,
    lengths_ref,
    tpo_ref,
    tmo_ref,
    leaf_ref,
    bins_ref,
    tp_ref,
    tm_ref,
    grad_ref,
    cols_ref,
    pk_ref,
    bins_bf,
    sums,
    turn,
    pair_g,
    pair_h,
    send_sem,
    recv_sem,
):
    nq, npos = scores_ref.shape
    me = lax.axis_index("doc")
    peers = [lax.rem(me + o, ndoc) for o in range(ndoc)]
    barrier = pltpu.get_barrier_semaphore()
    for o in range(1, ndoc):
        pl.semaphore_signal(barrier, inc=1, device_id={"doc": peers[o]}, device_id_type=MESH)

    def send(kind, o, src, dst):
        return pltpu.make_async_remote_copy(
            src_ref=src,
            dst_ref=dst,
            send_sem=send_sem.at[kind, o],
            recv_sem=recv_sem.at[kind, o],
            device_id={"doc": peers[o]},
            device_id_type=MESH,
        )

    def cast(p, carry):
        bins_bf[p] = bins_ref[p].astype(F32).astype(BF)
        return carry

    lax.fori_loop(0, ndoc, cast, 0)
    pl.semaphore_wait(barrier, ndoc - 1)
    col_copies = [send(0, o, bins_bf.at[peers[o]], cols_ref.at[me]) for o in range(1, ndoc)]
    for copy in col_copies:
        copy.start()
    cols_ref[me] = bins_bf[me]

    place = lax.broadcasted_iota(jnp.int32, (nq, npos), 1)
    shown = place < lengths_ref[...]
    clicked = jnp.logical_and(shown, clicks_ref[...] == 1)
    skipped = jnp.logical_and(shown, clicks_ref[...] == 0)
    code = jnp.where(clicked, 1.0, jnp.where(skipped, -1.0, 0.0)).astype(F32)
    count = jnp.sum(jnp.where(clicked, 1.0, 0.0), axis=1, keepdims=True)
    to_log2 = 1.4426950408889634
    disc_row = 1.0 / (jnp.log(2.0 + lax.broadcasted_iota(jnp.int32, (8, npos), 1).astype(F32)) * to_log2)
    disc_row = disc_row[0:1]
    ideal = jnp.sum(jnp.where(place.astype(F32) < count, disc_row, 0.0), axis=1, keepdims=True)
    gain = 1.0 / jnp.maximum(ideal, 1.0)
    weigh = jnp.where(clicked, 1.0 / tpo_ref[...], 1.0 / tmo_ref[...])
    turn[...] = jnp.zeros_like(turn)
    turn[0:nq] = scores_ref[...]
    turn[16 : 16 + nq] = code
    turn[32 : 32 + nq] = weigh
    turn[48:49] = disc_row
    stood = turn[...].T
    gap = jnp.abs(stood[:, 48:49] - disc_row)
    plus_row = jnp.zeros((1, npos), F32)
    minus_row = jnp.zeros((1, npos), F32)
    for q in range(nq):
        code_col = stood[:, 16 + q : 17 + q]
        code_row = code[q : q + 1]
        away = jnp.where(code_col * code_row < 0.0, gap, 0.0)
        y = code_col * (scores_ref[q : q + 1, :] - stood[:, q : q + 1])
        e = jnp.exp(-jnp.abs(y))
        inv = 1.0 / (1.0 + e)
        small = e * (1.0 - e * (0.5 - e * (1.0 / 3.0)))
        soft = jnp.maximum(y, 0.0) + jnp.where(e < 0.01, small, jnp.log(1.0 + e))
        loss = jnp.sum(away * soft * stood[:, 32 + q : 33 + q], axis=0, keepdims=True)
        loss = loss * gain[q : q + 1]
        plus_row = plus_row + jnp.where(code_row > 0.0, loss, 0.0)
        minus_row = minus_row + jnp.where(code_row < 0.0, loss, 0.0)
        scaled = away * inv
        pair_g[q] = code_col * scaled * jnp.where(y >= 0.0, 1.0, e)
        pair_h[q] = scaled * inv * e
    sums[me, 0:1] = plus_row
    sums[me, 1:2] = minus_row
    sum_copies = [send(1, o, sums.at[me], sums.at[me]) for o in range(1, ndoc)]
    for copy in sum_copies:
        copy.start()
    for copy in sum_copies:
        copy.wait()
    total = jnp.sum(sums[...], axis=0)
    t_new = jnp.sqrt(total / total[:, 0:1])
    tp_ref[...] = t_new[0:1]
    tm_ref[...] = t_new[1:2]
    t_inv = 1.0 / t_new
    unit = jnp.where(clicked, t_inv[0:1], t_inv[1:2])
    turn[0:nq] = unit
    unit_col = turn[...].T
    unit_row = unit * gain
    for q in range(nq):
        lanes = slice(q * npos, (q + 1) * npos)
        side = unit_col[:, q : q + 1]
        slope = jnp.sum(pair_g[q] * side, axis=0, keepdims=True) * unit_row[q : q + 1]
        curve = jnp.sum(pair_h[q] * side, axis=0, keepdims=True) * unit_row[q : q + 1]
        both = jnp.concatenate([slope, curve], axis=0)
        grad_ref[:, lanes] = both
        leaf_row = leaf_ref[:, lanes].astype(F32)
        pk_ref[me, :, lanes] = jnp.concatenate([both, leaf_row], axis=0).astype(BF)
    pk_copies = [send(2, o, pk_ref.at[me], pk_ref.at[me]) for o in range(1, ndoc)]
    for copy in pk_copies:
        copy.start()
    for copy in pk_copies + col_copies:
        copy.wait()


def hist_kernel(cols_ref, pk_ref, out_ref, w_ref, scale_ref):
    step = pl.program_id(0)
    nfeat, rows = cols_ref.shape[1], cols_ref.shape[2]

    @pl.when(step == 0)
    def _():
        out_ref[...] = jnp.zeros_like(out_ref)
        top = jnp.max(jnp.abs(pk_ref[:, 0:2, :].astype(F32)), axis=0)
        top = jnp.maximum(jnp.max(top, axis=1, keepdims=True), 1e-30)
        power = jnp.clip(jnp.floor(jnp.log(top) * 1.4426950408889634), -110.0, 110.0).astype(jnp.int32)
        power = jnp.broadcast_to(power, (2, 128))
        size, tiny = jnp.abs(power), power < 0
        up = jnp.full((2, 128), 128.0, F32)
        down = jnp.full((2, 128), 1.0 / 128.0, F32)
        for bit in range(7):
            on = ((size >> bit) & 1) == 1
            large, less = F32(2.0 ** (2**bit)), F32(2.0 ** -(2**bit))
            up = up * jnp.where(on, jnp.where(tiny, large, less), F32(1.0))
            down = down * jnp.where(on, jnp.where(tiny, less, large), F32(1.0))
        scale_ref[0:2] = up
        scale_ref[2:4] = down

    pack = pk_ref[step]
    leaf = pack[2:3]
    value = (pack[0:2].astype(F32) * scale_ref[0:2, 0:1]).astype(BF)
    high = value.astype(F8).astype(BF)
    low = (value - high) * BF(16.0)
    levels = lax.broadcasted_iota(jnp.int32, (LEAVES, rows), 0).astype(BF)
    hit = levels == leaf
    none = jnp.zeros((), BF)
    w_ref[...] = jnp.concatenate(
        [jnp.where(hit, part, none) for part in (high[0:1], high[1:2], low[0:1], low[1:2])], axis=0
    ).astype(F8)
    bins = lax.broadcasted_iota(jnp.int32, (BINS, rows), 0).astype(BF)
    for f in range(nfeat):
        one_hot = jnp.where(cols_ref[0, f : f + 1, :] == bins, jnp.ones((), BF), none).astype(F8)
        got = lax.dot_general(w_ref[...], one_hot, NT, preferred_element_type=F32)
        out_ref[f] += got[: 2 * LEAVES] + got[2 * LEAVES :] * (1.0 / 16.0)

    @pl.when(step == pl.num_programs(0) - 1)
    def _():
        for f in range(nfeat):
            out_ref[f, :LEAVES] *= scale_ref[2:3, 0:1]
            out_ref[f, LEAVES:] *= scale_ref[3:4, 0:1]


def body(scores, clicks, lengths, t_plus_old, t_minus_old, leaf, bins):
    ndoc = lax.axis_size("doc")
    nq, npos = scores.shape
    rows = leaf.shape[0]
    nfeat = bins.shape[0] // ndoc
    vmem = pl.BlockSpec(memory_space=pltpu.VMEM)
    t_plus, t_minus, gradients, cols, packs = pl.pallas_call(
        functools.partial(rows_kernel, ndoc),
        out_shape=(
            jax.ShapeDtypeStruct((1, npos), F32),
            jax.ShapeDtypeStruct((1, npos), F32),
            jax.ShapeDtypeStruct((2, rows), F32),
            jax.ShapeDtypeStruct((ndoc, nfeat, rows), BF),
            jax.ShapeDtypeStruct((ndoc, 3, rows), BF),
        ),
        in_specs=[vmem] * 7,
        out_specs=(vmem,) * 5,
        scratch_shapes=[
            pltpu.VMEM((ndoc, nfeat, rows), BF),
            pltpu.VMEM((ndoc, 2, npos), F32),
            pltpu.VMEM((npos, npos), F32),
            pltpu.VMEM((nq, npos, npos), F32),
            pltpu.VMEM((nq, npos, npos), F32),
            pltpu.SemaphoreType.DMA((3, ndoc)),
            pltpu.SemaphoreType.DMA((3, ndoc)),
        ],
        compiler_params=pltpu.CompilerParams(
            collective_id=0, has_side_effects=True, vmem_limit_bytes=40 << 20
        ),
    )(
        scores,
        clicks,
        lengths.reshape(nq, 1),
        t_plus_old.reshape(1, npos),
        t_minus_old.reshape(1, npos),
        leaf.reshape(1, rows),
        bins.reshape(ndoc, nfeat, rows),
    )
    hist = pl.pallas_call(
        hist_kernel,
        grid=(ndoc,),
        out_shape=jax.ShapeDtypeStruct((nfeat, 2 * LEAVES, BINS), F32),
        in_specs=[
            pl.BlockSpec((1, nfeat, rows), lambda i: (i, 0, 0)),
            pl.BlockSpec((ndoc, 3, rows), lambda i: (0, 0, 0)),
        ],
        out_specs=pl.BlockSpec((nfeat, 2 * LEAVES, BINS), lambda i: (0, 0, 0)),
        scratch_shapes=[pltpu.VMEM((4 * LEAVES, rows), F8), pltpu.VMEM((4, 128), F32)],
        compiler_params=pltpu.CompilerParams(vmem_limit_bytes=40 << 20),
    )(cols, packs)
    return (t_plus.reshape(npos), t_minus.reshape(npos), gradients, hist)


def solution(mesh):
    placed = (P("doc", None), P("doc", None), P("doc"), P(), P(), P("doc"), P("feat", "doc"))
    return jax.shard_map(
        body,
        mesh=mesh,
        in_specs=placed,
        out_specs=(P(), P(), P(None, "doc"), P(("feat", "doc"), None, None)),
        check_vma=False,
    )
```

time: 133 us -> 43 us (0.32)
  blocking collectives: 77.2 us -> 0 us
  matrix products: 41.3 us -> 0 us
  Pallas kernels: 0 us -> 37.9 us
  starting transfers between devices: 7.28 us -> 0 us
  other arithmetic: 4.7 us -> 0 us
  local copies, waits for them, and re-layouts: 1.17 us -> 4.14 us
    dot_general x3 -> x0, matrix products: 41.3 us -> none  [block_hist(): jnp.einsum('gr,nbr->ngb', weights, one_hot, preferred_element_type=jnp.fl...]
    psum x1 -> x0, blocking collectives: 41.1 us -> none  [body(): plus_sum, minus_sum = lax.psum((plus_part, minus_part), ('doc', 'feat'))]
    pallas_call x0 -> x2, Pallas kernels: none -> 37.9 us  [the longest x1 21.6 us: body(): pl.pallas_call(functools.partial(rows_kernel, ndoc), out_shape=(jax.Shape...]
    all_gather x2 -> x0, blocking collectives: 36 us -> none  [the longest x1 30.5 us: body(): piece = lax.all_gather(packed, 'doc', axis=1, tiled=True)]
    all_to_all x1 -> x0, starting transfers between devices: 7.28 us -> none  [body(): lax.all_to_all(bins.astype(jnp.bfloat16), 'doc', split_axis=0, concat_axi...]
    unnamed x17 -> x15, local copies, waits for them, and re-layouts: 1 us -> 3.33 us
    convert_element_type x7 -> x0, other arithmetic: 1.97 us -> none  [the longest x1 1.95 us: body(): bins.astype(jnp.bfloat16)]
    reduce_sum x4 -> x0, other arithmetic: 1.74 us -> none  [the longest x1 0.9 us: pair_terms(): clicks_count = jnp.sum(clicked, axis=1)]
  transfers between devices with their start and end apart: 1 -> 0, of which waited for: 0 -> 0; matrix products, arithmetic and copies ran while one was open for 2% -> 0% of each run, Pallas kernels for 0% -> 0%
where the time goes in v1:
time: 43 us; the launch traced here: 42.7 us
  Pallas kernels  37.9 us (88%)
  local copies, waits for them, and re-layouts  4.14 us (10%)
  between operations  0.68 us (2%)
    pallas_call x1, Pallas kernels, body(): pl.pallas_call(functools.partial(rows_kernel, ndoc), out_shape=(jax.Shape...  21.6 us
    pallas_call x1, Pallas kernels, body(): pl.pallas_call(hist_kernel, grid=(ndoc,), out_shape=jax.ShapeDtypeStruct(...  16.4 us
    unnamed x15, local copies, waits for them, and re-layouts  3.33 us

profile of v1, /device:TPU:0, one launch (start us, length us, event | category | flops | bytes accessed | tf_op | source)
XLA Modules:
  0.0 42.7 jit_solution(11457996431251206541)
XLA Ops:
  0.6 0.0 copy-start.5
  0.6 0.0 copy-start.1
  0.7 0.0 copy-start.2
  0.7 0.7 %reshape.32.leaf_ref = s32[1,1536]{1,0:T(1,128)S(1)} reshape(s32[1536]{0:T(1024)} %param.12) | data formatting | bytes 12288 | tf_op jit(solution)/shard_map/reshape | solution.py:219
  1.4 0.0 copy-done.5
  1.4 0.0 copy-start.3
  1.4 0.0 copy-start.4
  1.4 0.1 copy.11.lengths_ref
  1.5 0.0 copy-done.1
  1.5 0.0 copy-done.2
  1.5 0.5 %copy-done.3 = f32[128]{0:T(128)S(1)} copy-done((f32[128]{0:T(128)S(1)}, f32[128]{0:T(128)}, u32[]{:S(2)}) %copy-start.3) | copy-done | bytes 536
  2.0 0.0 copy-done.4
  2.1 0.0 copy-start
  2.1 1.1 %copy-done = s32[128,1536]{1,0:T(8,128)S(1)} copy-done((s32[128,1536]{1,0:T(8,128)S(1)}, s32[128,1536]{1,0:T(8,128)}, u32[]{:S(2)}) %copy-start) | copy-done | bytes 786456
  3.2 21.6 %shard_map.102 = (f32[1,128]{1,0:T(1,128)S(1)}, f32[1,128]{1,0:T(1,128)S(1)}, f32[2,1536]{1,0:T(2,128)S(1)}, bf16[8,16,1536]{2,1,0:T(8,128)(2,1)S(1)}, bf16[8,3,1536]{2,1,0:T(4,128)(2,1)S(1)}) custom-call(f32[12,128]{1,0:T(8,128)S(1)} %copy-done.1, s32[12,128]{1,0:T(8,128)S(1)} %copy-done.2, s32[12,1]{1,0:T(8,128)S(1)} %copy.11.lengths_ref, ...), custom_call_target="tpu_custom_call" | custom-call | tf_op jit(solution)/shard_map/pallas_call | solution.py:190
  24.8 16.4 %shard_map.103 = f32[16,64,256]{2,1,0:T(8,128)} custom-call(bf16[8,16,1536]{2,1,0:T(8,128)(2,1)S(1)} %get-tuple-element.12.cols_ref, bf16[8,3,1536]{2,1,0:T(4,128)(2,1)S(1)} %get-tuple-element.13.pk_ref), custom_call_target="tpu_custom_call" | custom-call | tf_op jit(solution)/shard_map/pallas_call | solution.py:222
  41.1 0.5 %copy.15 = f32[128]{0:T(128)} copy(f32[128]{0:T(128)S(1)} %bitcast.10) | data formatting | bytes 1024
  41.6 0.5 %copy.16 = f32[128]{0:T(128)} copy(f32[128]{0:T(128)S(1)} %bitcast.9) | data formatting | bytes 1024
  42.1 0.6 %copy.17 = f32[2,1536]{1,0:T(2,128)} copy(f32[2,1536]{1,0:T(2,128)S(1)} %get-tuple-element.20) | data formatting | bytes 24576
Async XLA Ops:
  0.6 0.8 %copy-start.5 = (s32[12]{0:T(128)S(1)}, s32[12]{0:T(128)}, u32[]{:S(2)}) copy-start(s32[12]{0:T(128)} %param.9) | copy-start | bytes 148
  0.6 0.9 %copy-start.1 = (f32[12,128]{1,0:T(8,128)S(1)}, f32[12,128]{1,0:T(8,128)}, u32[]{:S(2)}) copy-start(f32[12,128]{1,0:T(8,128)} %scores_ref.1) | copy-start | bytes 18436
  0.7 0.8 %copy-start.2 = (s32[12,128]{1,0:T(8,128)S(1)}, s32[12,128]{1,0:T(8,128)}, u32[]{:S(2)}) copy-start(s32[12,128]{1,0:T(8,128)} %clicks_ref.1) | copy-start | bytes 18436
  1.4 0.7 %copy-start.3 = (f32[128]{0:T(128)S(1)}, f32[128]{0:T(128)}, u32[]{:S(2)}) copy-start(f32[128]{0:T(128)} %param.10) | copy-start | bytes 1540
  1.4 0.7 %copy-start.4 = (f32[128]{0:T(128)S(1)}, f32[128]{0:T(128)}, u32[]{:S(2)}) copy-start(f32[128]{0:T(128)} %param.11) | copy-start | bytes 1540
  2.1 1.1 %copy-start = (s32[128,1536]{1,0:T(8,128)S(1)}, s32[128,1536]{1,0:T(8,128)}, u32[]{:S(2)}) copy-start(s32[128,1536]{1,0:T(8,128)} %param.13) | copy-start | bytes 2359300

commit v2 on v1

--- a/solution.py
+++ b/solution.py
@@ -18,13 +18,13 @@
 
 def rows_kernel(
     ndoc,
-    scores_ref,
-    clicks_ref,
+    scores_in,
+    clicks_in,
     lengths_ref,
-    tpo_ref,
-    tmo_ref,
-    leaf_ref,
-    bins_ref,
+    tpo_in,
+    tmo_in,
+    leaf_in,
+    bins_in,
     tp_ref,
     tm_ref,
     grad_ref,
@@ -35,10 +35,29 @@
     turn,
     pair_g,
     pair_h,
+    scores_ref,
+    clicks_ref,
+    tpo_ref,
+    tmo_ref,
+    leaf_ref,
+    bins_ref,
     send_sem,
     recv_sem,
+    in_sem,
 ):
     nq, npos = scores_ref.shape
+    bins_load = pltpu.make_async_copy(bins_in, bins_ref, in_sem.at[0])
+    bins_load.start()
+    pairs = [
+        (scores_in, scores_ref),
+        (clicks_in, clicks_ref),
+        (tpo_in, tpo_ref),
+        (tmo_in, tmo_ref),
+        (leaf_in, leaf_ref),
+    ]
+    loads = [pltpu.make_async_copy(a, b, in_sem.at[1 + k]) for k, (a, b) in enumerate(pairs)]
+    for load in loads:
+        load.start()
     me = lax.axis_index("doc")
     peers = [lax.rem(me + o, ndoc) for o in range(ndoc)]
     barrier = pltpu.get_barrier_semaphore()
@@ -59,6 +78,7 @@
         bins_bf[p] = bins_ref[p].astype(F32).astype(BF)
         return carry
 
+    bins_load.wait()
     lax.fori_loop(0, ndoc, cast, 0)
     pl.semaphore_wait(barrier, ndoc - 1)
     col_copies = [send(0, o, bins_bf.at[peers[o]], cols_ref.at[me]) for o in range(1, ndoc)]
@@ -66,6 +86,8 @@
         copy.start()
     cols_ref[me] = bins_bf[me]
 
+    for load in loads:
+        load.wait()
     place = lax.broadcasted_iota(jnp.int32, (nq, npos), 1)
     shown = place < lengths_ref[...]
     clicked = jnp.logical_and(shown, clicks_ref[...] == 1)
@@ -126,7 +148,7 @@
         curve = jnp.sum(pair_h[q] * side, axis=0, keepdims=True) * unit_row[q : q + 1]
         both = jnp.concatenate([slope, curve], axis=0)
         grad_ref[:, lanes] = both
-        leaf_row = leaf_ref[:, lanes].astype(F32)
+        leaf_row = leaf_ref[lanes].astype(F32).reshape(1, npos)
         pk_ref[me, :, lanes] = jnp.concatenate([both, leaf_row], axis=0).astype(BF)
     pk_copies = [send(2, o, pk_ref.at[me], pk_ref.at[me]) for o in range(1, ndoc)]
     for copy in pk_copies:
@@ -135,13 +157,18 @@
         copy.wait()
 
 
-def hist_kernel(cols_ref, pk_ref, out_ref, w_ref, scale_ref):
+def hist_kernel(
+    cols_ref, pk_ref, tp_in, tm_in, grad_in, out_ref, tp_ref, tm_ref, grad_ref, w_ref, scale_ref
+):
     step = pl.program_id(0)
     nfeat, rows = cols_ref.shape[1], cols_ref.shape[2]
 
     @pl.when(step == 0)
     def _():
         out_ref[...] = jnp.zeros_like(out_ref)
+        tp_ref[...] = tp_in[...]
+        tm_ref[...] = tm_in[...]
+        grad_ref[...] = grad_in[...]
         top = jnp.max(jnp.abs(pk_ref[:, 0:2, :].astype(F32)), axis=0)
         top = jnp.maximum(jnp.max(top, axis=1, keepdims=True), 1e-30)
         power = jnp.clip(jnp.floor(jnp.log(top) * 1.4426950408889634), -110.0, 110.0).astype(jnp.int32)
@@ -186,6 +213,7 @@
     nq, npos = scores.shape
     rows = leaf.shape[0]
     nfeat = bins.shape[0] // ndoc
+    anyw = pl.BlockSpec(memory_space=pltpu.HBM)
     vmem = pl.BlockSpec(memory_space=pltpu.VMEM)
     t_plus, t_minus, gradients, cols, packs = pl.pallas_call(
         functools.partial(rows_kernel, ndoc),
@@ -196,7 +224,7 @@
             jax.ShapeDtypeStruct((ndoc, nfeat, rows), BF),
             jax.ShapeDtypeStruct((ndoc, 3, rows), BF),
         ),
-        in_specs=[vmem] * 7,
+        in_specs=[anyw, anyw, vmem, anyw, anyw, anyw, anyw],
         out_specs=(vmem,) * 5,
         scratch_shapes=[
             pltpu.VMEM((ndoc, nfeat, rows), BF),
@@ -204,8 +232,15 @@
             pltpu.VMEM((npos, npos), F32),
             pltpu.VMEM((nq, npos, npos), F32),
             pltpu.VMEM((nq, npos, npos), F32),
+            pltpu.VMEM((nq, npos), F32),
+            pltpu.VMEM((nq, npos), jnp.int32),
+            pltpu.VMEM((1, npos), F32),
+            pltpu.VMEM((1, npos), F32),
+            pltpu.VMEM((rows,), jnp.int32),
+            pltpu.VMEM((ndoc, nfeat, rows), jnp.int32),
             pltpu.SemaphoreType.DMA((3, ndoc)),
             pltpu.SemaphoreType.DMA((3, ndoc)),
+            pltpu.SemaphoreType.DMA((6,)),
         ],
         compiler_params=pltpu.CompilerParams(
             collective_id=0, has_side_effects=True, vmem_limit_bytes=40 << 20
@@ -216,21 +251,28 @@
         lengths.reshape(nq, 1),
         t_plus_old.reshape(1, npos),
         t_minus_old.reshape(1, npos),
-        leaf.reshape(1, rows),
+        leaf,
         bins.reshape(ndoc, nfeat, rows),
     )
-    hist = pl.pallas_call(
+    whole = [pl.BlockSpec(a.shape, lambda i: (0, 0)) for a in (t_plus, t_minus, gradients)]
+    hist, t_plus, t_minus, gradients = pl.pallas_call(
         hist_kernel,
         grid=(ndoc,),
-        out_shape=jax.ShapeDtypeStruct((nfeat, 2 * LEAVES, BINS), F32),
+        out_shape=(
+            jax.ShapeDtypeStruct((nfeat, 2 * LEAVES, BINS), F32),
+            jax.ShapeDtypeStruct(t_plus.shape, F32),
+            jax.ShapeDtypeStruct(t_minus.shape, F32),
+            jax.ShapeDtypeStruct(gradients.shape, F32),
+        ),
         in_specs=[
             pl.BlockSpec((1, nfeat, rows), lambda i: (i, 0, 0)),
             pl.BlockSpec((ndoc, 3, rows), lambda i: (0, 0, 0)),
+            *whole,
         ],
-        out_specs=pl.BlockSpec((nfeat, 2 * LEAVES, BINS), lambda i: (0, 0, 0)),
+        out_specs=(pl.BlockSpec((nfeat, 2 * LEAVES, BINS), lambda i: (0, 0, 0)), *whole),
         scratch_shapes=[pltpu.VMEM((4 * LEAVES, rows), F8), pltpu.VMEM((4, 128), F32)],
         compiler_params=pltpu.CompilerParams(vmem_limit_bytes=40 << 20),
-    )(cols, packs)
+    )(cols, packs, t_plus, t_minus, gradients)
     return (t_plus.reshape(npos), t_minus.reshape(npos), gradients, hist)
 
 

time: 43 us -> 43 us (level)
    reshape x1 -> x0, local copies, waits for them, and re-layouts: 0.72 us -> none  [body(): leaf.reshape(1, rows)]
    reshape x1, local copies, waits for them, and re-layouts: 0.1 us -> 0.76 us  [body(): lengths.reshape(nq, 1)]
    unnamed x15 -> x12, local copies, waits for them, and re-layouts: 3.33 us -> 3.15 us
where the time goes in v2:
time: 43 us; the launch traced here: 42.7 us
  Pallas kernels  38.1 us (89%)
  local copies, waits for them, and re-layouts  3.9 us (9%)
  between operations  0.66 us (2%)
    pallas_call x1, Pallas kernels, body(): pl.pallas_call(functools.partial(rows_kernel, ndoc), out_shape=(jax.Shape...  21.7 us
    pallas_call x1, Pallas kernels, body(): pl.pallas_call(hist_kernel, grid=(ndoc,), out_shape=(jax.ShapeDtypeStruct...  16.4 us
    unnamed x12, local copies, waits for them, and re-layouts  3.15 us

profile of v2, /device:TPU:0, one launch (start us, length us, event | category | flops | bytes accessed | tf_op | source)
XLA Modules:
  0.0 42.7 jit_solution(1306587677801266126)
XLA Ops:
  0.6 0.0 copy-start.2
  0.6 0.0 copy-start.1
  0.7 0.8 %copy.11.lengths_ref = s32[12,1]{1,0:T(8,128)S(1)} copy(s32[12,1]{0,1:T(1,128)} %bitcast.9) | data formatting | bytes 96 | tf_op jit(solution)/shard_map/reshape | solution.py:251
  1.4 0.0 copy-done.2
  1.4 0.0 copy-done.1
  1.4 0.0 copy-start
  1.4 1.1 %copy-done = s32[128,1536]{1,0:T(8,128)S(1)} copy-done((s32[128,1536]{1,0:T(8,128)S(1)}, s32[128,1536]{1,0:T(8,128)}, u32[]{:S(2)}) %copy-start) | copy-done | bytes 786456
  2.5 0.0 copy-start.3
  2.5 0.7 %copy-done.3 = s32[1536]{0:T(1024)S(1)} copy-done((s32[1536]{0:T(1024)S(1)}, s32[1536]{0:T(1024)}, u32[]{:S(2)}) %copy-start.3) | copy-done | bytes 6168
  3.2 0.0 copy-start.4
  3.2 0.7 %copy-done.4 = f32[128]{0:T(128)S(1)} copy-done((f32[128]{0:T(128)S(1)}, f32[128]{0:T(128)}, u32[]{:S(2)}) %copy-start.4) | copy-done | bytes 536
  3.9 0.0 copy-start.5
  3.9 0.7 %copy-done.5 = f32[128]{0:T(128)S(1)} copy-done((f32[128]{0:T(128)S(1)}, f32[128]{0:T(128)}, u32[]{:S(2)}) %copy-start.5) | copy-done | bytes 536
  4.6 21.7 %shard_map.102 = (f32[1,128]{1,0:T(1,128)S(1)}, f32[1,128]{1,0:T(1,128)S(1)}, f32[2,1536]{1,0:T(2,128)S(1)}, bf16[8,16,1536]{2,1,0:T(8,128)(2,1)S(1)}, bf16[8,3,1536]{2,1,0:T(4,128)(2,1)S(1)}) custom-call(f32[12,128]{1,0:T(8,128)S(1)} %copy-done.1, s32[12,128]{1,0:T(8,128)S(1)} %copy-done.2, s32[12,1]{1,0:T(8,128)S(1)} %copy.11.lengths_ref, ...), custom_call_target="tpu_custom_call" | custom-call | tf_op jit(solution)/shard_map/pallas_call | solution.py:218
  26.3 16.4 %shard_map.103 = (f32[16,64,256]{2,1,0:T(8,128)}, f32[1,128]{1,0:T(1,128)}, f32[1,128]{1,0:T(1,128)}, f32[2,1536]{1,0:T(2,128)}) custom-call(bf16[8,16,1536]{2,1,0:T(8,128)(2,1)S(1)} %get-tuple-element.13.cols_ref, bf16[8,3,1536]{2,1,0:T(4,128)(2,1)S(1)} %get-tuple-element.14.pk_ref, f32[1,128]{1,0:T(1,128)S(1)} %get-tuple-element.15.tp_in, ...), custom_call_target="tpu_custom_call" | custom-call | tf_op jit(solution)/shard_map/pallas_call | solution.py:258
Async XLA Ops:
  0.6 0.8 %copy-start.2 = (s32[12,128]{1,0:T(8,128)S(1)}, s32[12,128]{1,0:T(8,128)}, u32[]{:S(2)}) copy-start(s32[12,128]{1,0:T(8,128)} %clicks_in.1) | copy-start | bytes 18436
  0.6 0.8 %copy-start.1 = (f32[12,128]{1,0:T(8,128)S(1)}, f32[12,128]{1,0:T(8,128)}, u32[]{:S(2)}) copy-start(f32[12,128]{1,0:T(8,128)} %scores_in.1) | copy-start | bytes 18436
  1.4 1.1 %copy-start = (s32[128,1536]{1,0:T(8,128)S(1)}, s32[128,1536]{1,0:T(8,128)}, u32[]{:S(2)}) copy-start(s32[128,1536]{1,0:T(8,128)} %param.13) | copy-start | bytes 2359300
  2.5 0.7 %copy-start.3 = (s32[1536]{0:T(1024)S(1)}, s32[1536]{0:T(1024)}, u32[]{:S(2)}) copy-start(s32[1536]{0:T(1024)} %leaf_in.1) | copy-start | bytes 18436
  3.2 0.7 %copy-start.4 = (f32[128]{0:T(128)S(1)}, f32[128]{0:T(128)}, u32[]{:S(2)}) copy-start(f32[128]{0:T(128)} %param.10) | copy-start | bytes 1540
  3.9 0.7 %copy-start.5 = (f32[128]{0:T(128)S(1)}, f32[128]{0:T(128)}, u32[]{:S(2)}) copy-start(f32[128]{0:T(128)} %param.11) | copy-start | bytes 1540

commit v3 on v2

--- a/solution.py
+++ b/solution.py
@@ -12,8 +12,62 @@
 F8 = jnp.float8_e4m3fn
 BF = jnp.bfloat16
 F32 = jnp.float32
+EARLY = 1
 MESH = pl.DeviceIdType.MESH
 NT = (((1,), (1,)), ((), ()))
+
+
+def partner(me, step, ndoc):
+    if ndoc & (ndoc - 1):
+        return lax.rem(step - me + ndoc, ndoc)
+    other = me
+    bit = 1
+    while bit < ndoc:
+        if step & bit:
+            other = other + (1 - 2 * ((me // bit) % 2)) * bit
+        bit *= 2
+    return other
+
+
+def power_scale(top, width):
+    power = jnp.floor(jnp.log(jnp.maximum(top, 1e-30)) * 1.4426950408889634)
+    power = jnp.broadcast_to(jnp.clip(power, -110.0, 110.0).astype(jnp.int32), (1, width))
+    size, tiny = jnp.abs(power), power < 0
+    up = jnp.full((1, width), 128.0, F32)
+    down = jnp.full((1, width), 1.0 / 128.0, F32)
+    for bit in range(7):
+        on = ((size >> bit) & 1) == 1
+        large, less = F32(2.0 ** (2**bit)), F32(2.0 ** -(2**bit))
+        up = up * jnp.where(on, jnp.where(tiny, large, less), F32(1.0))
+        down = down * jnp.where(on, jnp.where(tiny, less, large), F32(1.0))
+    return up, down
+
+
+def add_block(columns, pack, out_ref, w_ref):
+    nfeat, rows = out_ref.shape[0], pack.shape[1]
+    value, leaf = pack[0:2], pack[2:3]
+    high = value.astype(F8).astype(BF)
+    low = (value - high) * BF(16.0)
+    levels = lax.broadcasted_iota(jnp.int32, (LEAVES, rows), 0).astype(BF)
+    hit = levels == leaf
+    none = jnp.zeros((), BF)
+    w_ref[...] = jnp.concatenate(
+        [jnp.where(hit, part, none) for part in (high[0:1], high[1:2], low[0:1], low[1:2])], axis=0
+    ).astype(F8)
+    half_row = rows // 2
+    back = pack[3:4].astype(F32)
+    back = jnp.concatenate(
+        [
+            jnp.broadcast_to(back[:, 0:1], (LEAVES, 1)),
+            jnp.broadcast_to(back[:, half_row : half_row + 1], (LEAVES, 1)),
+        ],
+        axis=0,
+    )
+    bins = lax.broadcasted_iota(jnp.int32, (BINS, rows), 0).astype(BF)
+    for f in range(nfeat):
+        one_hot = jnp.where(columns(f) == bins, jnp.ones((), BF), none).astype(F8)
+        got = lax.dot_general(w_ref[...], one_hot, NT, preferred_element_type=F32)
+        out_ref[f] += (got[: 2 * LEAVES] + got[2 * LEAVES :] * (1.0 / 16.0)) * back
 
 
 def rows_kernel(
@@ -30,6 +84,8 @@
     grad_ref,
     cols_ref,
     pk_ref,
+    acc_ref,
+    w_ref,
     bins_bf,
     sums,
     turn,
@@ -59,20 +115,24 @@
     for load in loads:
         load.start()
     me = lax.axis_index("doc")
-    peers = [lax.rem(me + o, ndoc) for o in range(ndoc)]
+    half = max(ndoc // 2, 1)
+    peers = [partner(me, o, ndoc) for o in range(ndoc)]
     barrier = pltpu.get_barrier_semaphore()
     for o in range(1, ndoc):
         pl.semaphore_signal(barrier, inc=1, device_id={"doc": peers[o]}, device_id_type=MESH)
 
-    def send(kind, o, src, dst):
+    def send_any(kind, o, src, dst, peer=peers[-1]):
         return pltpu.make_async_remote_copy(
             src_ref=src,
             dst_ref=dst,
             send_sem=send_sem.at[kind, o],
             recv_sem=recv_sem.at[kind, o],
-            device_id={"doc": peers[o]},
+            device_id={"doc": peer},
             device_id_type=MESH,
         )
+
+    def send(kind, o, src, dst):
+        return send_any(kind, o, src, dst, peers[o])
 
     def cast(p, carry):
         bins_bf[p] = bins_ref[p].astype(F32).astype(BF)
@@ -81,10 +141,11 @@
     bins_load.wait()
     lax.fori_loop(0, ndoc, cast, 0)
     pl.semaphore_wait(barrier, ndoc - 1)
-    col_copies = [send(0, o, bins_bf.at[peers[o]], cols_ref.at[me]) for o in range(1, ndoc)]
-    for copy in col_copies:
+    col_copies = [send(0, o, bins_bf.at[peers[o]], cols_ref.at[o]) for o in range(1, ndoc)]
+    for copy in col_copies[:EARLY]:
         copy.start()
-    cols_ref[me] = bins_bf[me]
+    cols_ref[0] = bins_bf[me]
+    acc_ref[...] = jnp.zeros_like(acc_ref)
 
     for load in loads:
         load.wait()
@@ -141,71 +202,66 @@
     turn[0:nq] = unit
     unit_col = turn[...].T
     unit_row = unit * gain
+    slopes, curves = [], []
     for q in range(nq):
         lanes = slice(q * npos, (q + 1) * npos)
         side = unit_col[:, q : q + 1]
         slope = jnp.sum(pair_g[q] * side, axis=0, keepdims=True) * unit_row[q : q + 1]
         curve = jnp.sum(pair_h[q] * side, axis=0, keepdims=True) * unit_row[q : q + 1]
-        both = jnp.concatenate([slope, curve], axis=0)
-        grad_ref[:, lanes] = both
+        grad_ref[:, lanes] = jnp.concatenate([slope, curve], axis=0)
+        slopes.append(slope)
+        curves.append(curve)
+
+    def largest(values):
+        top = jnp.abs(values[0])
+        for value in values[1:]:
+            top = jnp.maximum(top, jnp.abs(value))
+        return jnp.max(top, axis=1, keepdims=True)
+
+    slope_up, slope_down = power_scale(largest(slopes), npos)
+    curve_up, curve_down = power_scale(largest(curves), npos)
+    for q in range(nq):
+        lanes = slice(q * npos, (q + 1) * npos)
         leaf_row = leaf_ref[lanes].astype(F32).reshape(1, npos)
-        pk_ref[me, :, lanes] = jnp.concatenate([both, leaf_row], axis=0).astype(BF)
-    pk_copies = [send(2, o, pk_ref.at[me], pk_ref.at[me]) for o in range(1, ndoc)]
+        down = slope_down if q < nq // 2 else curve_down
+        pk_ref[0, :, lanes] = jnp.concatenate(
+            [slopes[q] * slope_up, curves[q] * curve_up, leaf_row, down], axis=0
+        ).astype(BF)
+    pk_copies = [send(2, o, pk_ref.at[0], pk_ref.at[o]) for o in range(1, ndoc)]
     for copy in pk_copies:
         copy.start()
+    for copy in col_copies[EARLY:]:
+        copy.start()
+
+    def add(o):
+        add_block(lambda f: cols_ref[o, f : f + 1, :], pk_ref[o], acc_ref, w_ref)
+
+    add(0)
+
+    def arrived(o, carry):
+        send_any(2, o, pk_ref.at[0], pk_ref.at[o]).wait_recv()
+        send_any(0, o, bins_bf.at[0], cols_ref.at[o]).wait_recv()
+        add(o)
+        return carry
+
+    lax.fori_loop(1, half, arrived, 0)
+    for copy in pk_copies[half - 1 :] + col_copies[half - 1 :]:
+        copy.wait_recv()
     for copy in pk_copies + col_copies:
-        copy.wait()
+        copy.wait_send()
 
 
 def hist_kernel(
-    cols_ref, pk_ref, tp_in, tm_in, grad_in, out_ref, tp_ref, tm_ref, grad_ref, w_ref, scale_ref
+    cols_ref, pk_ref, acc_in, tp_in, tm_in, grad_in, out_ref, tp_ref, tm_ref, grad_ref, w_ref
 ):
-    step = pl.program_id(0)
-    nfeat, rows = cols_ref.shape[1], cols_ref.shape[2]
-
-    @pl.when(step == 0)
+    @pl.when(pl.program_id(0) == 0)
     def _():
-        out_ref[...] = jnp.zeros_like(out_ref)
+        out_ref[...] = acc_in[...]
         tp_ref[...] = tp_in[...]
         tm_ref[...] = tm_in[...]
         grad_ref[...] = grad_in[...]
-        top = jnp.max(jnp.abs(pk_ref[:, 0:2, :].astype(F32)), axis=0)
-        top = jnp.maximum(jnp.max(top, axis=1, keepdims=True), 1e-30)
-        power = jnp.clip(jnp.floor(jnp.log(top) * 1.4426950408889634), -110.0, 110.0).astype(jnp.int32)
-        power = jnp.broadcast_to(power, (2, 128))
-        size, tiny = jnp.abs(power), power < 0
-        up = jnp.full((2, 128), 128.0, F32)
-        down = jnp.full((2, 128), 1.0 / 128.0, F32)
-        for bit in range(7):
-            on = ((size >> bit) & 1) == 1
-            large, less = F32(2.0 ** (2**bit)), F32(2.0 ** -(2**bit))
-            up = up * jnp.where(on, jnp.where(tiny, large, less), F32(1.0))
-            down = down * jnp.where(on, jnp.where(tiny, less, large), F32(1.0))
-        scale_ref[0:2] = up
-        scale_ref[2:4] = down
-
-    pack = pk_ref[step]
-    leaf = pack[2:3]
-    value = (pack[0:2].astype(F32) * scale_ref[0:2, 0:1]).astype(BF)
-    high = value.astype(F8).astype(BF)
-    low = (value - high) * BF(16.0)
-    levels = lax.broadcasted_iota(jnp.int32, (LEAVES, rows), 0).astype(BF)
-    hit = levels == leaf
-    none = jnp.zeros((), BF)
-    w_ref[...] = jnp.concatenate(
-        [jnp.where(hit, part, none) for part in (high[0:1], high[1:2], low[0:1], low[1:2])], axis=0
-    ).astype(F8)
-    bins = lax.broadcasted_iota(jnp.int32, (BINS, rows), 0).astype(BF)
-    for f in range(nfeat):
-        one_hot = jnp.where(cols_ref[0, f : f + 1, :] == bins, jnp.ones((), BF), none).astype(F8)
-        got = lax.dot_general(w_ref[...], one_hot, NT, preferred_element_type=F32)
-        out_ref[f] += got[: 2 * LEAVES] + got[2 * LEAVES :] * (1.0 / 16.0)
-
-    @pl.when(step == pl.num_programs(0) - 1)
-    def _():
-        for f in range(nfeat):
-            out_ref[f, :LEAVES] *= scale_ref[2:3, 0:1]
-            out_ref[f, LEAVES:] *= scale_ref[3:4, 0:1]
+
+    add_block(lambda f: cols_ref[0, f : f + 1, :], pk_ref[0], out_ref, w_ref)
 
 
 def body(scores, clicks, lengths, t_plus_old, t_minus_old, leaf, bins):
@@ -213,20 +269,23 @@
     nq, npos = scores.shape
     rows = leaf.shape[0]
     nfeat = bins.shape[0] // ndoc
+    half = max(ndoc // 2, 1)
     anyw = pl.BlockSpec(memory_space=pltpu.HBM)
     vmem = pl.BlockSpec(memory_space=pltpu.VMEM)
-    t_plus, t_minus, gradients, cols, packs = pl.pallas_call(
+    t_plus, t_minus, gradients, cols, packs, acc = pl.pallas_call(
         functools.partial(rows_kernel, ndoc),
         out_shape=(
             jax.ShapeDtypeStruct((1, npos), F32),
             jax.ShapeDtypeStruct((1, npos), F32),
             jax.ShapeDtypeStruct((2, rows), F32),
             jax.ShapeDtypeStruct((ndoc, nfeat, rows), BF),
-            jax.ShapeDtypeStruct((ndoc, 3, rows), BF),
+            jax.ShapeDtypeStruct((ndoc, 4, rows), BF),
+            jax.ShapeDtypeStruct((nfeat, 2 * LEAVES, BINS), F32),
         ),
         in_specs=[anyw, anyw, vmem, anyw, anyw, anyw, anyw],
-        out_specs=(vmem,) * 5,
+        out_specs=(vmem,) * 6,
         scratch_shapes=[
+            pltpu.VMEM((4 * LEAVES, rows), F8),
             pltpu.VMEM((ndoc, nfeat, rows), BF),
             pltpu.VMEM((ndoc, 2, npos), F32),
             pltpu.VMEM((npos, npos), F32),
@@ -257,7 +316,7 @@
     whole = [pl.BlockSpec(a.shape, lambda i: (0, 0)) for a in (t_plus, t_minus, gradients)]
     hist, t_plus, t_minus, gradients = pl.pallas_call(
         hist_kernel,
-        grid=(ndoc,),
+        grid=(ndoc - half,),
         out_shape=(
             jax.ShapeDtypeStruct((nfeat, 2 * LEAVES, BINS), F32),
             jax.ShapeDtypeStruct(t_plus.shape, F32),
@@ -265,14 +324,15 @@
             jax.ShapeDtypeStruct(gradients.shape, F32),
         ),
         in_specs=[
-            pl.BlockSpec((1, nfeat, rows), lambda i: (i, 0, 0)),
-            pl.BlockSpec((ndoc, 3, rows), lambda i: (0, 0, 0)),
+            pl.BlockSpec((1, nfeat, rows), lambda i: (i + half, 0, 0)),
+            pl.BlockSpec((1, 4, rows), lambda i: (i + half, 0, 0)),
+            pl.BlockSpec((nfeat, 2 * LEAVES, BINS), lambda i: (0, 0, 0)),
             *whole,
         ],
         out_specs=(pl.BlockSpec((nfeat, 2 * LEAVES, BINS), lambda i: (0, 0, 0)), *whole),
-        scratch_shapes=[pltpu.VMEM((4 * LEAVES, rows), F8), pltpu.VMEM((4, 128), F32)],
+        scratch_shapes=[pltpu.VMEM((4 * LEAVES, rows), F8)],
         compiler_params=pltpu.CompilerParams(vmem_limit_bytes=40 << 20),
-    )(cols, packs, t_plus, t_minus, gradients)
+    )(cols, packs, acc, t_plus, t_minus, gradients)
     return (t_plus.reshape(npos), t_minus.reshape(npos), gradients, hist)
 
 

time: 43 us -> 36.2 us (0.84)
  Pallas kernels: 38.1 us -> 31.3 us
    pallas_call x1, Pallas kernels: 16.4 us -> 8.27 us  [body(): pl.pallas_call(hist_kernel, grid=(ndoc - half,), out_shape=(jax.ShapeDtyp...]
    pallas_call x1, Pallas kernels: 21.7 us -> 23 us  [body(): pl.pallas_call(functools.partial(rows_kernel, ndoc), out_shape=(jax.Shape...]
where the time goes in v3:
time: 36.2 us; the launch traced here: 35.9 us
  Pallas kernels  31.3 us (86%)
  local copies, waits for them, and re-layouts  3.9 us (11%)
  between operations  0.66 us (2%)
    pallas_call x1, Pallas kernels, body(): pl.pallas_call(functools.partial(rows_kernel, ndoc), out_shape=(jax.Shape...  23 us
    pallas_call x1, Pallas kernels, body(): pl.pallas_call(hist_kernel, grid=(ndoc - half,), out_shape=(jax.ShapeDtyp...  8.27 us
    unnamed x12, local copies, waits for them, and re-layouts  3.15 us
    reshape x1, local copies, waits for them, and re-layouts, body(): lengths.reshape(nq, 1)  0.76 us

profile of v3, /device:TPU:0, one launch (start us, length us, event | category | flops | bytes accessed | tf_op | source)
XLA Modules:
  0.0 35.9 jit_solution(15335480995510013052)
XLA Ops:
  0.6 0.0 copy-start.2
  0.6 0.0 copy-start.1
  0.7 0.8 %copy.11.lengths_ref = s32[12,1]{1,0:T(8,128)S(1)} copy(s32[12,1]{0,1:T(1,128)} %bitcast.9) | data formatting | bytes 96 | tf_op jit(solution)/shard_map/reshape | solution.py:310
  1.4 0.0 copy-done.2
  1.4 0.0 copy-done.1
  1.4 0.0 copy-start
  1.4 1.1 %copy-done = s32[128,1536]{1,0:T(8,128)S(1)} copy-done((s32[128,1536]{1,0:T(8,128)S(1)}, s32[128,1536]{1,0:T(8,128)}, u32[]{:S(2)}) %copy-start) | copy-done | bytes 786456
  2.5 0.0 copy-start.3
  2.5 0.7 %copy-done.3 = s32[1536]{0:T(1024)S(1)} copy-done((s32[1536]{0:T(1024)S(1)}, s32[1536]{0:T(1024)}, u32[]{:S(2)}) %copy-start.3) | copy-done | bytes 6168
  3.2 0.0 copy-start.4
  3.2 0.7 %copy-done.4 = f32[128]{0:T(128)S(1)} copy-done((f32[128]{0:T(128)S(1)}, f32[128]{0:T(128)}, u32[]{:S(2)}) %copy-start.4) | copy-done | bytes 536
  3.9 0.0 copy-start.5
  3.9 0.7 %copy-done.5 = f32[128]{0:T(128)S(1)} copy-done((f32[128]{0:T(128)S(1)}, f32[128]{0:T(128)}, u32[]{:S(2)}) %copy-start.5) | copy-done | bytes 536
  4.6 23.0 %shard_map.102 = (f32[1,128]{1,0:T(1,128)S(1)}, f32[1,128]{1,0:T(1,128)S(1)}, f32[2,1536]{1,0:T(2,128)S(1)}, bf16[8,16,1536]{2,1,0:T(8,128)(2,1)S(1)}, bf16[8,4,...) custom-call(f32[12,128]{1,0:T(8,128)S(1)} %copy-done.1, s32[12,128]{1,0:T(8,128)S(1)} %copy-done.2, ...), custom_call_target="tpu_custom_call" | custom-call | tf_op jit(solution)/shard_map/pallas_call | solution.py:275
  27.6 8.3 %shard_map.103 = (f32[16,64,256]{2,1,0:T(8,128)}, f32[1,128]{1,0:T(1,128)}, f32[1,128]{1,0:T(1,128)}, f32[2,1536]{1,0:T(2,128)}) custom-call(bf16[8,16,1536]{2,1,0:T(8,128)(2,1)S(1)} %get-tuple-element.14.cols_ref, bf16[8,4,1536]{2,1,0:T(4,128)(2,1)S(1)} %get-tuple-element.15.pk_ref, f32[16,64,256]{2,1,0:T(8,128)S(1)} %get-tuple-element.16.acc_in, ...), custom_call_target="tpu_custom_call" | custom-call | tf_op jit(solution)/shard_map/pallas_call | solution.py:317
Async XLA Ops:
  0.6 0.8 %copy-start.2 = (s32[12,128]{1,0:T(8,128)S(1)}, s32[12,128]{1,0:T(8,128)}, u32[]{:S(2)}) copy-start(s32[12,128]{1,0:T(8,128)} %clicks_in.1) | copy-start | bytes 18436
  0.6 0.8 %copy-start.1 = (f32[12,128]{1,0:T(8,128)S(1)}, f32[12,128]{1,0:T(8,128)}, u32[]{:S(2)}) copy-start(f32[12,128]{1,0:T(8,128)} %scores_in.1) | copy-start | bytes 18436
  1.4 1.1 %copy-start = (s32[128,1536]{1,0:T(8,128)S(1)}, s32[128,1536]{1,0:T(8,128)}, u32[]{:S(2)}) copy-start(s32[128,1536]{1,0:T(8,128)} %param.13) | copy-start | bytes 2359300
  2.5 0.7 %copy-start.3 = (s32[1536]{0:T(1024)S(1)}, s32[1536]{0:T(1024)}, u32[]{:S(2)}) copy-start(s32[1536]{0:T(1024)} %leaf_in.1) | copy-start | bytes 18436
  3.2 0.7 %copy-start.4 = (f32[128]{0:T(128)S(1)}, f32[128]{0:T(128)}, u32[]{:S(2)}) copy-start(f32[128]{0:T(128)} %param.10) | copy-start | bytes 1540
  3.9 0.7 %copy-start.5 = (f32[128]{0:T(128)S(1)}, f32[128]{0:T(128)}, u32[]{:S(2)}) copy-start(f32[128]{0:T(128)} %param.11) | copy-start | bytes 1540
